TPU v7x, 32 devices: a whole 2x2x4 slice. The times are simulated.
32 devices in a mesh: qrow: 4 (over x, core), qcol: 4 (over z), grp: 2 (over y).
Axes of the slice: x: 2, y: 2, z: 4, core: 2. Of those that a mesh axis runs over, the one named last changes fastest.
Arguments:
- density: float32 [512, 3, 128, 128], P(('qrow', 'qcol', 'grp')), may hold values from -1 to 1.5, as said below
- pattern: int32 [512, 3], P(('qrow', 'qcol', 'grp')), may hold values from 0 to 1, as said below
- qm_sites: float32 [4, 512], P(None, ('qrow', 'qcol', 'grp')), may hold values from 0 to 8, as said below
- positions: float32 [3, 8, 8, 4, 128], P(None, 'qrow', 'qcol', 'grp'), may hold values from 0 to 1
- atom_types: int32 [8, 8, 4, 128], P('qrow', 'qcol', 'grp'), may hold values from 0 to 7
- charges: float32 [8, 8, 4, 128], P('qrow', 'qcol', 'grp'), may hold values from -4 to 4
- eps_table: float32 [8], replicated, may hold values from 0.2 to 2
- embed_atoms: int32 [32, 32, 128], P(('qrow', 'qcol', 'grp')), may hold values from 0 to 1023
- embed_counts: int32 [32, 32], P(('qrow', 'qcol', 'grp')), may hold values from 0 to 128, as said below
Outputs:
- purified: float32 [512, 3, 128, 128], P(('qrow', 'qcol', 'grp'))
- mm_force: float32 [3, 8, 8, 4, 128], P(None, 'qrow', 'qcol', 'grp')
Inputs may be any that keep to these rules, and one draw needn't show every extreme that they name: `pattern`: column 1 is 1 in every block row; column 0 is 1 in every block row i with i mod 16 < 1, and column 2 in every block row i with i mod 16 >= 15. `density`: dominant diagonal near 0.5 with small entries elsewhere. `qm_sites`: centres lie in the MM box; the fourth row lies in 0.2 to 0.8. `embed_counts`: one owner, drawn from the seed, receives 128 atoms from every device.
All inputs are finite; a program needn't handle non-finite values.
Results may differ from a plain program's by a relative error of at most 0.0003.
Values sent between devices are 32-bit elements; how exact they have to be, the bound alone decides.
A program may use at most 128 MiB of HBM per device.

v0:
```python
import functools
import math

import jax
import jax.numpy as jnp
from jax import lax
from jax.experimental import pallas as pl
from jax.experimental.pallas import tpu as pltpu
from jax.sharding import PartitionSpec as P

W = 1
ITERS = 6


SIGMA_SQ = 0.25
EMBED = 20.0
SOFTEN = 1.0
MESH = pl.DeviceIdType.MESH
K_STACK = True
AT_ONCE = 2
SCALE = math.sqrt(1.0 / (SIGMA_SQ * math.log(2.0)))


def padded(cells, sides, width):
    for axis, dim in sides:
        count = lax.axis_size(axis)
        head = lax.slice_in_dim(cells, 0, width, axis=dim)
        tail = lax.slice_in_dim(cells, cells.shape[dim] - width, cells.shape[dim], axis=dim)
        cells = jnp.concatenate(
            [
                lax.ppermute(tail, axis, [(i, (i + 1) % count) for i in range(count)]),
                cells,
                lax.ppermute(head, axis, [((i + 1) % count, i) for i in range(count)]),
            ],
            axis=dim,
        )
    return cells


def keep_of(pattern, first_row, total_rows):
    row_ids = first_row + jnp.arange(pattern.shape[0], dtype=jnp.int32)[:, None]
    column_ids = row_ids + jnp.arange(pattern.shape[1], dtype=jnp.int32)[None, :] - W
    inside = (column_ids >= 0) & (column_ids < total_rows) & (pattern > 0)
    return jnp.where(inside, 1.0, 0.0).astype(jnp.float32)


def split(value):
    high = value.astype(jnp.bfloat16)
    return high, (value - high.astype(jnp.float32)).astype(jnp.bfloat16)


def purify_kernel(
    sizes, keep_ref, density_ref, out_ref, diag_ref, high, low, outbox, inbox, send_sem, recv_sem
):
    rows, bs = density_ref.shape[0], density_ref.shape[2]
    n_col, n_grp = sizes[1], sizes[2]
    total = sizes[0] * n_col * n_grp
    me = (lax.axis_index("qrow") * n_col + lax.axis_index("qcol")) * n_grp + lax.axis_index("grp")
    has_prev, has_next = me > 0, me < total - 1

    def place(index):
        return (index // (n_col * n_grp), (index // n_grp) % n_col, index % n_grp)

    to_prev, to_next = place(jnp.maximum(me - 1, 0)), place(jnp.minimum(me + 1, total - 1))

    def copy_prev(s):
        return pltpu.make_async_remote_copy(
            outbox.at[s, 0], inbox.at[s, 1], send_sem.at[s, 0], recv_sem.at[s, 1],
            device_id=to_prev, device_id_type=MESH)

    def copy_next(s):
        return pltpu.make_async_remote_copy(
            outbox.at[s, 1], inbox.at[s, 0], send_sem.at[s, 1], recv_sem.at[s, 0],
            device_id=to_next, device_id_type=MESH)

    barrier = pltpu.get_barrier_semaphore()

    @pl.when(has_prev)
    def _():
        pl.semaphore_signal(barrier, inc=1, device_id=to_prev, device_id_type=MESH)

    @pl.when(has_next)
    def _():
        pl.semaphore_signal(barrier, inc=1, device_id=to_next, device_id_type=MESH)

    eye = lax.broadcasted_iota(jnp.int32, (bs, bs), 0) == lax.broadcasted_iota(jnp.int32, (bs, bs), 1)
    half = jnp.where(eye, 0.5, 0.0)

    def masked(i):
        blocks = [density_ref[i, e] * keep_ref[i, e] for e in range(3)]
        blocks[W] = blocks[W] - half
        for e in range(3):
            out_ref[i, e] = blocks[e]
        return jnp.concatenate(blocks, axis=1)

    def put(slot, row, value):
        high[slot, row], low[slot, row] = split(value)

    first, last = masked(0), masked(rows - 1)
    outbox[0, 0] = first[:, : 2 * bs]
    outbox[0, 1] = last[:, bs:]
    put(0, 1, first)
    put(0, rows, last)

    pl.semaphore_wait(barrier, jnp.where(has_prev, 1, 0) + jnp.where(has_next, 1, 0))

    def send(s):
        @pl.when(has_prev)
        def _():
            copy_prev(s).start()

        @pl.when(has_next)
        def _():
            copy_next(s).start()

    send(0)
    edge = jnp.zeros((bs, 3 * bs), jnp.bfloat16)
    for slot in range(2):
        for row in (0, rows + 1):
            high[slot, row] = edge
            low[slot, row] = edge

    def fill(i, carry):
        put(0, i + 1, masked(i))
        return carry

    lax.fori_loop(1, rows - 1, fill, 0)

    def product(left, windows):
        left_high, left_low = left
        parts = []
        for tile in range(2):
            columns = slice(tile * bs, (tile + 2) * bs)
            wide_high, wide_low = windows[tile]
            if K_STACK:
                deep = jnp.concatenate([left_high[:, columns], left_low[:, columns], left_high[:, columns]], axis=1)
                wide = jnp.concatenate([wide_high, wide_high, wide_low], axis=0)
                parts.append(jnp.dot(deep, wide, preferred_element_type=jnp.float32))
            else:
                both = jnp.concatenate([left_high[:, columns], left_low[:, columns]], axis=0)
                by_high = jnp.dot(both, wide_high, preferred_element_type=jnp.float32)
                by_low = jnp.dot(left_high[:, columns], wide_low, preferred_element_type=jnp.float32)
                parts.append(by_high[:bs] + (by_high[bs:] + by_low))
        return [parts[0][:, :bs], parts[0][:, bs:] + parts[1][:, :bs], parts[1][:, bs:]]

    def window(store, slot, i):
        before, here, after = store.at[slot, i], store.at[slot, i + 1], store.at[slot, i + 2]
        one = jnp.concatenate([before[:, bs:], here[:, : 2 * bs]], axis=0)
        none = jnp.zeros((bs, bs), jnp.bfloat16)
        top = jnp.concatenate([none, here[:, 2 * bs :]], axis=1)
        return one, jnp.concatenate([top, after[:, : 2 * bs]], axis=0)

    def some_rows(slot, picked):
        windows = [list(zip(window(high, slot, i), window(low, slot, i))) for i in picked]
        keeps = [[keep_ref[i, e] for e in range(3)] for i in picked]
        squares = []
        for i, pieces, keep in zip(picked, windows, keeps):
            blocks = product((high[slot, i + 1], low[slot, i + 1]), pieces)
            squares.append(split(jnp.concatenate([keep[e] * blocks[e] for e in range(3)], axis=1)))
        cubes = [product(square, pieces) for square, pieces in zip(squares, windows)]
        results = []
        for i, cube, keep in zip(picked, cubes, keeps):
            fresh = [1.5 * out_ref[i, e] - (2.0 * keep[e]) * cube[e] for e in range(3)]
            results.append((fresh, split(jnp.concatenate(fresh, axis=1))))
        for i, (fresh, (fresh_high, fresh_low)) in zip(picked, results):
            for e in range(3):
                out_ref[i, e] = fresh[e]
            high[1 - slot, i + 1] = fresh_high
            low[1 - slot, i + 1] = fresh_low
        return [jnp.concatenate(fresh, axis=1) for fresh, _ in results]

    steps = (rows - 2) // AT_ONCE

    def sweep(s, carry):
        slot = lax.rem(s, 2)

        def inner(i, c):
            some_rows(slot, [1 + AT_ONCE * i + k for k in range(AT_ONCE)])
            return c

        lax.fori_loop(0, steps // 2, inner, 0)

        @pl.when(has_prev)
        def _():
            copy_prev(s).wait_send()
            copy_next(s).wait_recv()
            high[slot, 0, :, bs:], low[slot, 0, :, bs:] = split(inbox[s, 0])

        @pl.when(has_next)
        def _():
            copy_next(s).wait_send()
            copy_prev(s).wait_recv()
            high[slot, rows + 1, :, : 2 * bs], low[slot, rows + 1, :, : 2 * bs] = split(inbox[s, 1])

        top, bottom = some_rows(slot, [0, rows - 1])

        @pl.when(s < ITERS - 1)
        def _():
            outbox[s + 1, 0] = top[:, : 2 * bs]
            outbox[s + 1, 1] = bottom[:, bs:]
            send(s + 1)

        lax.fori_loop(steps // 2, steps, inner, 0)
        return carry

    lax.fori_loop(0, ITERS, sweep, 0)

    def diagonal(i, carry):
        block = out_ref[i, W] + half
        out_ref[i, W] = block
        diag_ref[i] = jnp.sum(jnp.where(eye, block, 0.0), axis=0, keepdims=True)
        return carry

    lax.fori_loop(0, rows, diagonal, 0)


def purify(density, keep_mask, sizes):
    rows, band, bs = density.shape[:3]
    vmem, smem = pl.BlockSpec(memory_space=pltpu.VMEM), pl.BlockSpec(memory_space=pltpu.SMEM)
    return pl.pallas_call(
        functools.partial(purify_kernel, sizes),
        out_shape=(
            jax.ShapeDtypeStruct(density.shape, jnp.float32),
            jax.ShapeDtypeStruct((rows, 1, bs), jnp.float32),
        ),
        in_specs=[smem, vmem],
        out_specs=(vmem, vmem),
        scratch_shapes=[
            pltpu.VMEM((2, rows + 2, bs, band * bs), jnp.bfloat16),
            pltpu.VMEM((2, rows + 2, bs, band * bs), jnp.bfloat16),
            pltpu.VMEM((ITERS, 2, bs, (band - 1) * bs), jnp.float32),
            pltpu.VMEM((ITERS, 2, bs, (band - 1) * bs), jnp.float32),
            pltpu.SemaphoreType.DMA((ITERS, 2)),
            pltpu.SemaphoreType.DMA((ITERS, 2)),
        ],
        compiler_params=pltpu.CompilerParams(
            collective_id=0, has_side_effects=True, vmem_limit_bytes=40 * 1024 * 1024
        ),
        cost_estimate=pl.CostEstimate(
            flops=2 * 3 * 8 * 2 * ITERS * rows * bs**3, bytes_accessed=8 * density.size, transcendentals=0
        ),
    )(keep_mask, density)


def pair_kernel(cells, around_ref, own_ref, strength_ref, out_ref, spread):
    cells_x, cells_y, cells_z = cells
    atoms = own_ref.shape[2]
    step_y = cells_z + 2
    step_x = step_y * (cells_y + 2)
    ones = jnp.ones((8, atoms), jnp.float32)
    group = 32

    def one_cell(cell, carry):
        cx, cy, cz = cell // (cells_y * cells_z), (cell // cells_z) % cells_y, cell % cells_z
        corner = cx * step_x + cy * step_y + cz
        for axis in range(3):
            row = own_ref[axis, pl.ds(cell, 1), :]
            spread[axis] = jnp.transpose(jnp.broadcast_to(row, (atoms, atoms)))

        def one_group(g, c):
            here = pl.ds(pl.multiple_of(g * group, group), group)
            mine = [spread[axis, here, :] for axis in range(3)]
            sums = [jnp.zeros((group, atoms), jnp.float32) for _ in range(3)]
            for dx in range(3):
                for dy in range(3):
                    for dz in range(3):
                        at = pl.ds(corner + dx * step_x + dy * step_y + dz, 1)
                        gap = [mine[axis] - around_ref[axis, at, :] for axis in range(3)]
                        power = around_ref[3, at, :] - (gap[0] * gap[0] + gap[1] * gap[1] + gap[2] * gap[2])
                        weight = jnp.exp2(power)
                        sums = [sums[axis] + weight * gap[axis] for axis in range(3)]
            for axis in range(3):
                spread[3 + axis, here, :] = sums[axis]
            return c

        lax.fori_loop(0, atoms // group, one_group, 0)
        strength = strength_ref[pl.ds(cell, 1), :] * (1.0 / SCALE)
        for axis in range(3):
            summed = lax.dot_general(
                ones, spread[3 + axis], (((1,), (1,)), ((), ())),
                precision=lax.Precision.HIGHEST, preferred_element_type=jnp.float32)
            out_ref[axis, pl.ds(cell, 1), :] = summed[:1] * strength
        return carry

    lax.fori_loop(0, cells_x * cells_y * cells_z, one_cell, 0)


def embed_kernel(per_owner, list_ref, table_ref, coords_ref, charge_ref, pair_ref, out_ref):
    cells, atoms = charge_ref.shape
    slots = list_ref.shape[1]
    cell_ids = lax.broadcasted_iota(jnp.int32, (16, slots), 0)
    atom_ids = lax.broadcasted_iota(jnp.int32, (atoms, slots), 0)

    def one_owner(owner, sums):
        row = list_ref[pl.ds(owner, 1), :]
        in_cell = jnp.where(cell_ids == (row >> int(math.log2(atoms))), 1.0, 0.0).astype(jnp.bfloat16)
        in_slot = jnp.where(atom_ids == (row & (atoms - 1)), 1.0, 0.0).astype(jnp.bfloat16)
        times = lax.dot_general(in_cell, in_slot, (((1,), (1,)), ((), ())), preferred_element_type=jnp.float32)
        sums = list(sums)
        for part in range(per_owner // 8):
            start = pl.ds(pl.multiple_of(owner * per_owner + part * 8, 8), 8)
            table = table_ref[start, :]
            site = [jnp.broadcast_to(table[:, k : k + 1], (8, atoms)) for k in range(4)]
            for cell in range(cells):
                gap = [coords_ref[axis, cell : cell + 1, :] - site[axis] for axis in range(3)]
                square = gap[0] * gap[0] + gap[1] * gap[1] + gap[2] * gap[2] + SOFTEN
                root = lax.rsqrt(square)
                factor = (site[3] * times[cell : cell + 1, :]) * (root * root * root)
                for axis in range(3):
                    sums[axis * cells + cell] = sums[axis * cells + cell] + factor * gap[axis]
        return tuple(sums)

    zero = jnp.zeros((8, atoms), jnp.float32)
    sums = lax.fori_loop(0, list_ref.shape[0], one_owner, (zero,) * (3 * cells))
    for axis in range(3):
        for cell in range(cells):
            force = jnp.sum(sums[axis * cells + cell], axis=0, keepdims=True)
            out_ref[axis, cell : cell + 1, :] = (
                pair_ref[axis, cell : cell + 1, :] + EMBED * charge_ref[cell : cell + 1, :] * force
            )


def per_device(
    density, pattern, qm_sites, positions, atom_types, charges, eps_table, embed_atoms, embed_counts
):
    row_count = density.shape[0]
    axes = ("qrow", "qcol", "grp")
    sizes = tuple(lax.axis_size(axis) for axis in axes)
    device_count = sizes[0] * sizes[1] * sizes[2]
    first_row = lax.axis_index(axes) * row_count
    keep_mask = keep_of(pattern, first_row, row_count * device_count)
    grid_shape = positions.shape[1:]
    cells, atoms = grid_shape[:3], grid_shape[3]
    cell_count = cells[0] * cells[1] * cells[2]
    flat = (cell_count, atoms)

    type_ids = jnp.arange(eps_table.shape[0], dtype=jnp.int32)[:, None, None, None, None]
    strength = jnp.sqrt(
        jnp.sum(
            jnp.where(atom_types[None] == type_ids, eps_table[:, None, None, None, None], 0.0),
            axis=0,
        )
    )
    stacked = jnp.concatenate([positions, jnp.log2(strength)[None]], axis=0)
    extended = padded(stacked, (("qrow", 1), ("qcol", 2), ("grp", 3)), 1)
    wide = extended.shape[1:]
    around = jnp.concatenate(
        [
            jnp.stack(
                [
                    (extended[axis] + (lax.broadcasted_iota(jnp.int32, wide, axis) - 1).astype(jnp.float32)) * SCALE
                    for axis in range(3)
                ]
            ),
            extended[3:],
        ],
        axis=0,
    ).reshape(4, -1, atoms)
    local = [lax.broadcasted_iota(jnp.int32, grid_shape, axis) for axis in range(3)]
    own = jnp.stack([(positions[axis] + local[axis].astype(jnp.float32)) * SCALE for axis in range(3)])
    coords = jnp.stack(
        [
            positions[axis] + (local[axis] + lax.axis_index(axes[axis]) * cells[axis]).astype(jnp.float32)
            for axis in range(3)
        ]
    ).reshape((3,) + flat)

    keep_mask, around = lax.optimization_barrier((keep_mask, around))
    current, diagonal = purify(density, keep_mask, sizes)
    qm_charge = qm_sites[3] - jnp.mean(diagonal[:, 0], axis=1)
    table = jnp.concatenate([qm_sites[:3], qm_charge[None]], axis=0).T
    table = lax.all_to_all(
        jnp.broadcast_to(table.reshape(1, -1), (device_count, table.size)), axes, 0, 0, tiled=True
    ).reshape(-1, 4)

    pair = pl.pallas_call(
        functools.partial(pair_kernel, cells),
        out_shape=jax.ShapeDtypeStruct((3,) + flat, jnp.float32),
        scratch_shapes=[pltpu.VMEM((6, atoms, atoms), jnp.float32)],
        compiler_params=pltpu.CompilerParams(vmem_limit_bytes=16 * 1024 * 1024),
        cost_estimate=pl.CostEstimate(
            flops=27 * 15 * cell_count * atoms * atoms, bytes_accessed=4 * around.size,
            transcendentals=27 * cell_count * atoms * atoms,
        ),
    )(around, own.reshape((3,) + flat), strength.reshape(flat))

    live = jnp.arange(embed_atoms.shape[2], dtype=jnp.int32)[None, :] < embed_counts[0][:, None]
    lists = jnp.where(live, embed_atoms[0], -1)
    force = pl.pallas_call(
        functools.partial(embed_kernel, row_count),
        out_shape=jax.ShapeDtypeStruct((3,) + flat, jnp.float32),
        compiler_params=pltpu.CompilerParams(vmem_limit_bytes=16 * 1024 * 1024),
    )(lists, table, coords, charges.reshape(flat), pair)
    return (current, force.reshape(positions.shape))


def solution(mesh):
    in_specs = (
        P(("qrow", "qcol", "grp"), None, None, None),
        P(("qrow", "qcol", "grp"), None),
        P(None, ("qrow", "qcol", "grp")),
        P(None, "qrow", "qcol", "grp", None),
        P("qrow", "qcol", "grp", None),
        P("qrow", "qcol", "grp", None),
        P(),
        P(("qrow", "qcol", "grp"), None, None),
        P(("qrow", "qcol", "grp"), None),
    )
    out_specs = (P(("qrow", "qcol", "grp"), None, None, None), P(None, "qrow", "qcol", "grp", None))
    return jax.shard_map(
        per_device, mesh=mesh, in_specs=in_specs, out_specs=out_specs, check_vma=False
    )
```

profile of v0, /device:TPU:0, one launch (start us, length us, event | category | flops | bytes accessed | tf_op | source)
XLA Modules:
  0.0 100.7 jit_solution(17596592250411065391)
XLA Ops:
  0.6 0.8 select_reduce_fusion
  1.4 0.7 fusion.3
  2.2 0.5 collective-permute-start
  2.7 2.0 %collective-permute-start.1 = (f32[4,1,2,2,128]{4,3,2,1,0:T(2,128)S(1)}, f32[4,1,2,2,128]{4,3,2,1,0:T(2,128)S(1)}, u32[]{:S(2)}, u32[]{:S(2)}) collective-permute-start(f32[4,1,2,2,128]{4,3,2,1,0:T(2,128)S(1)} %get-tuple-element.19), channel_id=1, source_target_pairs={{8,0},{16,8},{24,16},{0,24},{9,1},{17,9},{25,17},{1,25},{10,2},{18... | collective-permute-start | bytes 24584 | tf_op jit(solution)/shard_map/ppermute | solution.py:33
  4.7 0.8 copy.17
  5.4 0.8 bitcast_select_fusion.list_ref
  6.2 0.8 add_multiply_fusion.2
  7.0 0.1 fusion.8.keep_ref
  7.1 0.0 collective-permute-done
  7.1 0.0 collective-permute-done.1
  7.1 0.7 pad_maximum_fusion.3
  7.9 2.4 %collective-permute-start.2 = (f32[4,4,1,2,128]{4,3,2,1,0:T(2,128)S(1)}, f32[4,4,1,2,128]{4,3,2,1,0:T(2,128)S(1)}, u32[]{:S(2)}, u32[]{:S(2)}) collective-permute-start(f32[4,4,1,2,128]{4,3,2,1,0:T(2,128)S(1)} %get-tuple-element.16), channel_id=1, source_target_pairs={{0,2},{2,4},{4,6},{6,0},{1,3},{3,5},{5,7},{7,1},{8,10},{10,12},{12... | collective-permute-start | bytes 49160 | tf_op jit(solution)/shard_map/ppermute | solution.py:31
  10.2 2.1 %collective-permute-start.3 = (f32[4,4,1,2,128]{4,3,2,1,0:T(2,128)S(1)}, f32[4,4,1,2,128]{4,3,2,1,0:T(2,128)S(1)}, u32[]{:S(2)}, u32[]{:S(2)}) collective-permute-start(f32[4,4,1,2,128]{4,3,2,1,0:T(2,128)S(1)} %get-tuple-element.17), channel_id=1, source_target_pairs={{2,0},{4,2},{6,4},{0,6},{3,1},{5,3},{7,5},{1,7},{10,8},{12,10},{14... | collective-permute-start | bytes 49160 | tf_op jit(solution)/shard_map/ppermute | solution.py:33
  12.3 1.8 %collective-permute-done.2 = f32[4,4,1,2,128]{4,3,2,1,0:T(2,128)S(1)} collective-permute-done((f32[4,4,1,2,128]{4,3,2,1,0:T(2,128)S(1)}, f32[4,4,1,2,128]{4,3,2,1,0:T(2,128)S(1)}, u32[]{:S(2)}, u32[]{:S(2)}) %collective-permute-start.2) | collective-permute-done | bytes 16416 | tf_op jit(solution)/shard_map/ppermute | solution.py:31
  14.1 0.1 collective-permute-done.3
  14.2 0.7 pad_maximum_fusion.2
  14.9 0.1 fusion.9
  15.0 1.7 %collective-permute-start.4 = (f32[4,4,4,1,128]{4,3,2,1,0:T(1,128)S(1)}, f32[4,4,4,1,128]{4,3,2,1,0:T(1,128)S(1)}, u32[]{:S(2)}, u32[]{:S(2)}) collective-permute-start(f32[4,4,4,1,128]{4,3,2,1,0:T(1,128)S(1)} %get-tuple-element.14), channel_id=1, source_target_pairs={{0,1},{1,0},{2,3},{3,2},{4,5},{5,4},{6,7},{7,6},{8,9},{9,8},{10,11... | collective-permute-start | bytes 98312 | tf_op jit(solution)/shard_map/ppermute | solution.py:31
  16.6 0.4 collective-permute-start.5
  17.1 1.9 %collective-permute-done.4 = f32[4,4,4,1,128]{4,3,2,1,0:T(1,128)S(1)} collective-permute-done((f32[4,4,4,1,128]{4,3,2,1,0:T(1,128)S(1)}, f32[4,4,4,1,128]{4,3,2,1,0:T(1,128)S(1)}, u32[]{:S(2)}, u32[]{:S(2)}) %collective-permute-start.4) | collective-permute-done | bytes 32800 | tf_op jit(solution)/shard_map/ppermute | solution.py:31
  19.0 1.5 %collective-permute-done.5 = f32[4,4,4,1,128]{4,3,2,1,0:T(1,128)S(1)} collective-permute-done((f32[4,4,4,1,128]{4,3,2,1,0:T(1,128)S(1)}, f32[4,4,4,1,128]{4,3,2,1,0:T(1,128)S(1)}, u32[]{:S(2)}, u32[]{:S(2)}) %collective-permute-start.5) | collective-permute-done | bytes 32800 | tf_op jit(solution)/shard_map/ppermute | solution.py:33
  20.5 0.8 pad_maximum_fusion
  21.3 0.1 fusion.2
  21.5 0.0 copy-start.1
  21.5 1.9 %copy-done.1 = f32[16,3,128,128]{3,2,1,0:T(8,128)S(1)} copy-done((f32[16,3,128,128]{3,2,1,0:T(8,128)S(1)}, f32[16,3,128,128]{3,2,1,0:T(8,128)}, u32[]{:S(2)}) %copy-start.1) | copy-done | bytes 3145752
  23.3 0.0 copy-start.2
  23.3 44.6 %shard_map.104 = (f32[16,3,128,128]{3,2,1,0:T(8,128)S(1)}, f32[16,1,128]{2,1,0:T(1,128)S(1)}) custom-call(f32[16,3]{1,0:T(8,128)S(1)} %fusion.8.keep_ref, f32[16,3,128,128]{3,2,1,0:T(8,128)S(1)} %copy-done.1), custom_call_target="tpu_custom_call" | custom-call | flops 19327352832 | bytes 6291456 | tf_op jit(solution)/shard_map/pallas_call | solution.py:220
  67.9 0.2 reduce_sum.19
  68.1 0.0 copy-done.2
  68.2 0.1 copy.18
  68.3 0.1 broadcast_in_dim.44
  68.3 0.6 broadcast_in_dim.45
  69.0 9.3 %all-to-all-start = ((f32[32,1,64]{2,1,0:T(1,128)}), f32[32,1,64]{2,1,0:T(1,128)S(1)}, u32[]{:S(2)}, u32[]{:S(2)}) async-start(f32[32,1,64]{2,1,0:T(1,128)} %broadcast_in_dim.45), calls=%async_computation | async-start | bytes 32768 | tf_op jit(solution)/shard_map/all_to_all | solution.py:372
  78.3 0.0 copy-start
  78.3 13.0 %shard_map.105.pair_ref = f32[3,8,128]{2,1,0:T(8,128)S(1)} custom-call(f32[4,64,128]{2,1,0:T(8,128)S(1)} %pad_maximum_fusion.1.around_ref, f32[3,8,128]{2,1,0:T(8,128)S(1)} %pad_maximum_fusion.5.own_ref, f32[8,128]{1,0:T(8,128)S(1)} %bitcast.24), custom_call_target="tpu_custom_call" | custom-call | flops 53084160 | bytes 131072 | tf_op jit(solution)/shard_map/pallas_call | solution.py:376
  91.3 0.0 all-to-all-done
  91.3 0.5 broadcast.110
  91.9 0.7 reduce.4
  92.6 0.2 reshape.69.table_ref
  92.7 0.0 copy-done
  92.7 6.3 %shard_map.106 = f32[3,8,128]{2,1,0:T(8,128)} custom-call(s32[32,128]{1,0:T(8,128)S(1)} %bitcast_select_fusion.list_ref, f32[512,4]{1,0:T(8,128)S(1)} %reshape.69.table_ref, f32[3,8,128]{2,1,0:T(8,128)S(1)} %pad_maximum_fusion.4.coords_ref, f32[8,128]{1,0:T(8,128)S(1)} %bitcast.23, f32[3,8,128]{2,1,0:T(8,128)S(1)} %shard_map.105.pair_ref), custom_call_target="tpu_custom_call" | custom-call | tf_op jit(solution)/shard_map/pallas_call | solution.py:389
  99.0 1.7 %copy.20 = f32[16,3,128,128]{3,2,1,0:T(8,128)} copy(f32[16,3,128,128]{3,2,1,0:T(8,128)S(1)} %get-tuple-element.34) | data formatting | bytes 6291456
  (11 shorter events, 0.1 us)
Async XLA Ops:
  2.2 4.9 %collective-permute-start = (f32[4,1,2,2,128]{4,3,2,1,0:T(2,128)S(1)}, f32[4,1,2,2,128]{4,3,2,1,0:T(2,128)S(1)}, u32[]{:S(2)}, u32[]{:S(2)}) collective-permute-start(f32[4,1,2,2,128]{4,3,2,1,0:T(2,128)S(1)} %get-tuple-element.18), channel_id=1, source_target_pairs={{0,8},{8,16},{16,24},{24,0},{1,9},{9,17},{17,25},{25,1},{2,10},{10... | collective-permute-start | bytes 24584 | tf_op jit(solution)/shard_map/ppermute | solution.py:31
  2.7 4.4 %collective-permute-start.1 = (f32[4,1,2,2,128]{4,3,2,1,0:T(2,128)S(1)}, f32[4,1,2,2,128]{4,3,2,1,0:T(2,128)S(1)}, u32[]{:S(2)}, u32[]{:S(2)}) collective-permute-start(f32[4,1,2,2,128]{4,3,2,1,0:T(2,128)S(1)} %get-tuple-element.19), channel_id=1, source_target_pairs={{8,0},{16,8},{24,16},{0,24},{9,1},{17,9},{25,17},{1,25},{10,2},{18... | collective-permute-start | bytes 24584 | tf_op jit(solution)/shard_map/ppermute | solution.py:33
  7.9 6.2 %collective-permute-start.2 = (f32[4,4,1,2,128]{4,3,2,1,0:T(2,128)S(1)}, f32[4,4,1,2,128]{4,3,2,1,0:T(2,128)S(1)}, u32[]{:S(2)}, u32[]{:S(2)}) collective-permute-start(f32[4,4,1,2,128]{4,3,2,1,0:T(2,128)S(1)} %get-tuple-element.16), channel_id=1, source_target_pairs={{0,2},{2,4},{4,6},{6,0},{1,3},{3,5},{5,7},{7,1},{8,10},{10,12},{12... | collective-permute-start | bytes 49160 | tf_op jit(solution)/shard_map/ppermute | solution.py:31
  10.2 3.9 %collective-permute-start.3 = (f32[4,4,1,2,128]{4,3,2,1,0:T(2,128)S(1)}, f32[4,4,1,2,128]{4,3,2,1,0:T(2,128)S(1)}, u32[]{:S(2)}, u32[]{:S(2)}) collective-permute-start(f32[4,4,1,2,128]{4,3,2,1,0:T(2,128)S(1)} %get-tuple-element.17), channel_id=1, source_target_pairs={{2,0},{4,2},{6,4},{0,6},{3,1},{5,3},{7,5},{1,7},{10,8},{12,10},{14... | collective-permute-start | bytes 49160 | tf_op jit(solution)/shard_map/ppermute | solution.py:33
  15.0 4.0 %collective-permute-start.4 = (f32[4,4,4,1,128]{4,3,2,1,0:T(1,128)S(1)}, f32[4,4,4,1,128]{4,3,2,1,0:T(1,128)S(1)}, u32[]{:S(2)}, u32[]{:S(2)}) collective-permute-start(f32[4,4,4,1,128]{4,3,2,1,0:T(1,128)S(1)} %get-tuple-element.14), channel_id=1, source_target_pairs={{0,1},{1,0},{2,3},{3,2},{4,5},{5,4},{6,7},{7,6},{8,9},{9,8},{10,11... | collective-permute-start | bytes 98312 | tf_op jit(solution)/shard_map/ppermute | solution.py:31
  16.6 3.9 %collective-permute-start.5 = (f32[4,4,4,1,128]{4,3,2,1,0:T(1,128)S(1)}, f32[4,4,4,1,128]{4,3,2,1,0:T(1,128)S(1)}, u32[]{:S(2)}, u32[]{:S(2)}) collective-permute-start(f32[4,4,4,1,128]{4,3,2,1,0:T(1,128)S(1)} %get-tuple-element.15), channel_id=1, source_target_pairs={{1,0},{0,1},{3,2},{2,3},{5,4},{4,5},{7,6},{6,7},{9,8},{8,9},{11,10... | collective-permute-start | bytes 98312 | tf_op jit(solution)/shard_map/ppermute | solution.py:33
  21.5 1.9 %copy-start.1 = (f32[16,3,128,128]{3,2,1,0:T(8,128)S(1)}, f32[16,3,128,128]{3,2,1,0:T(8,128)}, u32[]{:S(2)}) copy-start(f32[16,3,128,128]{3,2,1,0:T(8,128)} %density_ref.1) | copy-start | bytes 9437188
  23.3 44.8 %copy-start.2 = (f32[4,16]{1,0:T(4,128)S(1)}, f32[4,16]{1,0:T(4,128)}, u32[]{:S(2)}) copy-start(f32[4,16]{1,0:T(4,128)} %param.11) | copy-start | bytes 772
  69.0 22.3 %all-to-all-start = ((f32[32,1,64]{2,1,0:T(1,128)}), f32[32,1,64]{2,1,0:T(1,128)S(1)}, u32[]{:S(2)}, u32[]{:S(2)}) async-start(f32[32,1,64]{2,1,0:T(1,128)} %broadcast_in_dim.45), calls=%async_computation | async-start | bytes 32768 | tf_op jit(solution)/shard_map/all_to_all | solution.py:372
  78.3 14.4 %copy-start = (f32[2,2,2,128]{3,2,1,0:T(2,128)S(1)}, f32[2,2,2,128]{3,2,1,0:T(2,128)}, u32[]{:S(2)}) copy-start(f32[2,2,2,128]{3,2,1,0:T(2,128)} %param.14) | copy-start | bytes 12292
where the time goes:
time: 101 us
  Pallas kernels  63.9 us (63%)
  starting transfers between devices  18.4 us (18%)
  other arithmetic  6.48 us (6%)
  local copies, waits for them, and re-layouts  5.88 us (6%)
  waiting for transfers between devices  5.29 us (5%)
    pallas_call x1, Pallas kernels, purify(): pl.pallas_call(functools.partial(purify_kernel, sizes), out_shape=(jax.Sh...  44.6 us
    pallas_call x1, Pallas kernels, per_device(): pl.pallas_call(functools.partial(pair_kernel, cells), out_shape=jax.Shape...  13 us
    all_to_all x1, starting transfers between devices, per_device(): lax.all_to_all(jnp.broadcast_to(table.reshape(1, -1), (device_count, tabl...  9.32 us
    pallas_call x1, Pallas kernels, per_device(): pl.pallas_call(functools.partial(embed_kernel, row_count), out_shape=jax....  6.31 us
    ppermute x3, starting transfers between devices, padded(): lax.ppermute(tail, axis, [(i, (i + 1) % count) for i in range(count)])  4.53 us
    ppermute x3, starting transfers between devices, padded(): lax.ppermute(head, axis, [((i + 1) % count, i) for i in range(count)])  4.52 us
    unnamed x8, local copies, waits for them, and re-layouts  4.32 us
    ppermute x3, waiting for transfers between devices, padded(): lax.ppermute(tail, axis, [(i, (i + 1) % count) for i in range(count)])  3.7 us
  transfers between devices with their start and end apart: 7, of which 4 were waited for; matrix products, arithmetic and copies ran while one was open for 2% of the time, Pallas kernels for 13%

commit v1 on v0

v1 whole, which is shorter than its diff:
```python
import functools
import math

import jax
import jax.numpy as jnp
from jax import lax
from jax.experimental import pallas as pl
from jax.experimental.pallas import tpu as pltpu
from jax.sharding import PartitionSpec as P

W = 1
ITERS = 6


SIGMA_SQ = 0.25
EMBED = 20.0
SOFTEN = 1.0
MESH = pl.DeviceIdType.MESH
SCALE = math.sqrt(1.0 / (SIGMA_SQ * math.log(2.0)))


def split(value):
    high = value.astype(jnp.bfloat16)
    return high, (value - high.astype(jnp.float32)).astype(jnp.bfloat16)


def step_kernel(
    sizes, pattern_ref, eps_ref, counts_ref, density_ref, sites_ref, positions_ref, types_ref, charges_ref, lists_ref,
    out_ref, force_ref,
    z0, z1, high0, high1, low0, low1, edge0, edge1, edge_keep, keep_ref,
    keep_out, keep_in, first_out, first_in, third_out, third_in, outbox, inbox,
    blocks_ref, sites_in, site_rows, around_ref, spread, pair_ref, times_ref, field_ref,
    diag_ref, charge_out, charge_in, charge_square, charge_rows,
    send_sem, recv_sem, load_sem, store_sem, block_send, block_recv, site_send, site_recv, charge_send, charge_recv
):
    rows, bs = density_ref.shape[0], density_ref.shape[2]
    n_row, n_col, n_grp = sizes
    total = n_row * n_col * n_grp
    at_row, at_col, at_grp = lax.axis_index("qrow"), lax.axis_index("qcol"), lax.axis_index("grp")
    home = at_row * n_col + at_col
    me = home * n_grp + at_grp
    has_prev, has_next = me > 0, me < total - 1

    def place(index):
        return (index // (n_col * n_grp), (index // n_grp) % n_col, index % n_grp)

    to_prev, to_next = place(jnp.maximum(me - 1, 0)), place(jnp.minimum(me + 1, total - 1))
    targets, present = (to_prev, to_next), (has_prev, has_next)
    full, high, low, edge = (z0, z1), (high0, high1), (low0, low1), (edge0, edge1)

    def message(pair, number, side):
        source, landing = pair
        return pltpu.make_async_remote_copy(
            source.at[side], landing.at[1 - side], send_sem.at[number, side], recv_sem.at[number, 1 - side],
            device_id=targets[side], device_id_type=MESH)

    def level_boxes(level):
        return outbox.at[level], inbox.at[level]

    def send(pair, number):
        for side in range(2):
            @pl.when(present[side])
            def _():
                message(pair, number, side).start()

    def finish(pair, number, side):
        message(pair, number, side).wait_send()
        message(pair, number, 1 - side).wait_recv()

    barrier = pltpu.get_barrier_semaphore()

    def greet(k, carry):
        pl.semaphore_signal(barrier, inc=1, device_id=place(lax.rem(me + k, total)), device_id_type=MESH)
        return carry

    lax.fori_loop(1, total, greet, 0)

    near_rows, far_rows = (0, rows - 1), (1, rows - 2)
    loads = [pltpu.make_async_copy(density_ref.at[i], z0.at[i], load_sem.at[k]) for k, i in enumerate(near_rows + far_rows)]
    loads.append(pltpu.make_async_copy(density_ref.at[pl.ds(2, rows - 4)], z0.at[pl.ds(2, rows - 4)], load_sem.at[4]))
    for load in loads:
        load.start()

    def keep_row(i, carry):
        for e in range(3):
            column = me * rows + i + e - W
            inside = (column >= 0) & (column < total * rows) & (pattern_ref[i, e] > 0)
            keep_ref[i, e] = jnp.where(inside, 1.0, 0.0).astype(jnp.float32)
        return carry

    lax.fori_loop(0, rows, keep_row, 0)

    cells, atoms = charges_ref.shape
    kinds = types_ref[...]
    eps = jnp.zeros((cells, atoms), jnp.float32)
    for kind in range(eps_ref.shape[0]):
        eps = jnp.where(kinds == kind, eps_ref[kind], eps)
    strength = jnp.sqrt(eps)
    for axis in range(3):
        blocks_ref[4, at_grp, axis] = positions_ref[axis]
    blocks_ref[4, at_grp, 3] = jnp.log2(strength)
    blocks_ref[4, at_grp, 4] = jnp.zeros((8, atoms), jnp.float32)
    blocks_ref[4, at_grp, 4, 0:4, 0:rows] = sites_ref[...]

    eye = lax.broadcasted_iota(jnp.int32, (bs, bs), 0) == lax.broadcasted_iota(jnp.int32, (bs, bs), 1)
    half = jnp.where(eye, 0.5, 0.0)

    def put(slot, row, value):
        high[slot][row + 2], low[slot][row + 2] = split(value)

    def masked(i):
        blocks = [z0[i, e] if e == W else z0[i, e] * keep_ref[i, e] for e in range(3)]
        blocks[W] = blocks[W] - half
        for e in range(3):
            z0[i, e] = blocks[e]
        return jnp.concatenate(blocks, axis=1)

    for load in loads[:4]:
        load.wait()
    near = [masked(0), masked(rows - 1)]
    far = [masked(1), masked(rows - 2)]
    cut = (slice(0, 2 * bs), slice(bs, 3 * bs))
    rest = (slice(2 * bs, 3 * bs), slice(0, bs))
    for side in range(2):
        first_out[side] = near[side][:, cut[side]]
        third_out[side] = near[side][:, rest[side]]
        outbox[0, side] = far[side][:, cut[side]]
        for e in range(3):
            keep_out[side, e : e + 1, :] = jnp.full((1, bs), keep_ref[(rows - 1) * side, e], jnp.float32)

    pl.semaphore_wait(barrier, total - 1)
    send((first_out, first_in), 0)
    send(level_boxes(0), 3)
    send((third_out, third_in), 1)
    send((keep_out, keep_in), 2)

    across = pltpu.make_async_remote_copy(
        blocks_ref.at[4, at_grp], blocks_ref.at[4, at_grp], block_send.at[4], block_recv.at[4],
        device_id=(at_row, at_col, 1 - at_grp), device_id_type=MESH)
    across_in = pltpu.make_async_remote_copy(
        blocks_ref.at[4, 1 - at_grp], blocks_ref.at[4, 1 - at_grp], block_send.at[4], block_recv.at[4],
        device_id=(at_row, at_col, 1 - at_grp), device_id_type=MESH)
    across.start()

    for side, row in ((0, 0), (1, rows - 1)):
        put(0, row, near[side])
    for side, row in ((0, 1), (1, rows - 2)):
        put(0, row, far[side])
    blank = jnp.zeros((bs, 3 * bs), jnp.bfloat16)
    for side in range(2):
        edge_keep[side] = jnp.zeros((8, bs), jnp.float32)
        edge0[side] = jnp.zeros((bs, 3 * bs), jnp.float32)
        for slot in range(2):
            for row in ((0, 1), (rows + 2, rows + 3))[side]:
                high[slot][row] = blank
                low[slot][row] = blank

    loads[4].wait()

    def fill(i, carry):
        put(0, i, masked(i))
        return carry

    lax.fori_loop(2, rows - 2, fill, 0)

    def product(left_high, left_low, windows):
        parts = []
        for tile in range(2):
            columns = slice(tile * bs, (tile + 2) * bs)
            wide_high, wide_low = windows[tile]
            deep = jnp.concatenate([left_high[:, columns], left_low[:, columns], left_high[:, columns]], axis=1)
            wide = jnp.concatenate([wide_high, wide_high, wide_low], axis=0)
            parts.append(jnp.dot(deep, wide, preferred_element_type=jnp.float32))
        return [parts[0][:, :bs], parts[0][:, bs:] + parts[1][:, :bs], parts[1][:, bs:]]

    def window(store, i):
        before, here, after = store[i + 1], store[i + 2], store[i + 3]
        one = jnp.concatenate([before[:, bs:], here[:, : 2 * bs]], axis=0)
        none = jnp.zeros((bs, bs), jnp.bfloat16)
        top = jnp.concatenate([none, here[:, 2 * bs :]], axis=1)
        return one, jnp.concatenate([top, after[:, : 2 * bs]], axis=0)

    def own(i):
        return -1 < i < rows

    def masks(i):
        if own(i):
            return [keep_ref[i, e] for e in range(3)]
        return [edge_keep[0 if i < 0 else 1, e : e + 1, :] for e in range(3)]

    def squared(slot, i, factor, keep):
        windows = list(zip(window(high[slot], i), window(low[slot], i)))
        blocks = product(high[slot][i + 2], low[slot][i + 2], windows)
        blocks = [blocks[e] * (factor if e == W else keep[e] * factor) for e in range(3)]
        return split(jnp.concatenate(blocks, axis=1))

    def finished(slot, i, square, keep):
        windows = list(zip(window(high[slot], i), window(low[slot], i)))
        cube = product(square[0], square[1], windows)
        fresh = []
        for e in range(3):
            columns = slice(e * bs, (e + 1) * bs)
            old = full[slot][i, e] if own(i) else edge[slot][0 if i < 0 else 1, :, columns]
            fresh.append(old - (cube[e] if e == W else keep[e] * cube[e]))
            if own(i):
                full[1 - slot][i, e] = fresh[e]
            else:
                edge[1 - slot][0 if i < 0 else 1, :, columns] = fresh[e]
        put(1 - slot, i, jnp.concatenate(fresh, axis=1))

    def run(tasks):
        kept = [masks(i) for _, i, _ in tasks]
        squares = [squared(slot, i, factor, keep) for (slot, i, factor), keep in zip(tasks, kept)]
        for (slot, i, _), square, keep in zip(tasks, squares, kept):
            finished(slot, i, square, keep)

    middle = list(range(4, rows - 4))
    outer = [1, rows - 2, 2, rows - 3, 3, rows - 4]

    def factor_of(level):
        return (4.0 / 3.0) * 2.25**level

    def post(level, slot):
        for side, row in ((0, 1), (1, rows - 2)):
            for k, e in enumerate(((0, 1), (1, 2))[side]):
                outbox[level, side, :, k * bs : (k + 1) * bs] = full[slot][row, e]
        send(level_boxes(level), 3 + level)

    def take_far(level, slot):
        for side in range(2):
            @pl.when(present[side])
            def _():
                finish(level_boxes(level), 3 + level, side)
                row = (0, rows + 3)[side]
                columns = cut[1 - side]
                high[slot][row, :, columns], low[slot][row, :, columns] = split(inbox[level, side])

    def around_copy(k):
        step_row, step_col = k // 3 - 1, k % 3 - 1
        target = (lax.rem(at_row + step_row + n_row, n_row), lax.rem(at_col + step_col + n_col, n_col), at_grp)
        return pltpu.make_async_remote_copy(
            blocks_ref.at[4], blocks_ref.at[8 - k], block_send.at[k], block_recv.at[8 - k],
            device_id=target, device_id_type=MESH)

    def site_copy(k, slot):
        peer = lax.rem(home + k, n_row * n_col)
        where = home if slot is None else peer
        return pltpu.make_async_remote_copy(
            sites_in.at[where], sites_in.at[where], site_send.at[k], site_recv.at[where],
            device_id=(peer // n_col, lax.rem(peer, n_col), at_grp), device_id_type=MESH)

    others = [k for k in range(9) if k != 4]

    def pass_on():
        across.wait_send()
        across_in.wait_recv()
        for k in others:
            around_copy(k).start()
        for g in range(n_grp):
            sites_in[home, g] = blocks_ref[4, g, 4]

        def one(k, carry):
            site_copy(k, None).start()
            return carry

        lax.fori_loop(1, n_row * n_col, one, 0)

    def gather_around():
        for k in others:
            around_copy(k).wait_send()
            around_copy(8 - k).wait_recv()
        for x in range(-1, 3):
            for y in range(-1, 3):
                for z in range(-1, 3):
                    k = (x // 2 + 1) * 3 + y // 2 + 1
                    g = at_grp if 0 <= z < 2 else 1 - at_grp
                    cell = (x % 2) * 4 + (y % 2) * 2 + z % 2
                    at = (x + 1) * 16 + (y + 1) * 4 + z + 1
                    for axis, shift in enumerate((x, y, z)):
                        row = blocks_ref[k, g, axis, cell : cell + 1, :]
                        around_ref[axis, at : at + 1, :] = (row + float(shift)) * SCALE
                    around_ref[3, at : at + 1, :] = blocks_ref[k, g, 3, cell : cell + 1, :]

    def gather_sites():
        def one(k, carry):
            site_copy(k, None).wait_send()
            site_copy(k, k).wait_recv()
            return carry

        lax.fori_loop(1, n_row * n_col, one, 0)
        per = bs // 8

        def some(n, carry):
            tiles = sites_in[pl.ds(n * (per // n_grp), per // n_grp)].reshape(bs, atoms)
            turned = jnp.transpose(tiles)[:rows]
            for j in range(per):
                at = pl.ds(pl.multiple_of((n * per + j) * rows, rows), rows)
                for axis in range(3):
                    site_rows[axis, at, :] = jnp.broadcast_to(turned[:, j * 8 + axis : j * 8 + axis + 1], (rows, atoms))
            return carry

        lax.fori_loop(0, total // per, some, 0)

    def count_atoms():
        cell_ids = lax.broadcasted_iota(jnp.int32, (16, atoms), 0)
        atom_ids = lax.broadcasted_iota(jnp.int32, (atoms, atoms), 0)
        slot_ids = lax.broadcasted_iota(jnp.int32, (1, atoms), 1)
        shift = int(math.log2(atoms))

        def some(n, carry):
            for j in range(4):
                owner = n * 4 + j
                row = jnp.where(slot_ids < counts_ref[owner], lists_ref[pl.ds(owner, 1), :], -1)
                in_cell = jnp.where(cell_ids == (row >> shift), 1.0, 0.0).astype(jnp.bfloat16)
                in_slot = jnp.where(atom_ids == (row & (atoms - 1)), 1.0, 0.0).astype(jnp.bfloat16)
                times_ref[owner] = lax.dot_general(
                    in_cell, in_slot, (((1,), (1,)), ((), ())), preferred_element_type=jnp.float32)[:cells]
            return carry

        lax.fori_loop(0, total // 4, some, 0)

    def make_field():
        spot = [
            [positions_ref[axis, cell : cell + 1, :] + ((at_row, at_col, at_grp)[axis] * 2 + (cell >> (2 - axis)) % 2).astype(jnp.float32)
             for cell in range(cells)]
            for axis in range(3)
        ]

        def one(n, carry):
            at = pl.ds(pl.multiple_of(n * 8, 8), 8)
            site = [site_rows[axis, at, :] for axis in range(3)]
            times = times_ref[n // (rows // 8)]
            for cell in range(cells):
                gap = [spot[axis][cell] - site[axis] for axis in range(3)]
                square = gap[0] * gap[0] + gap[1] * gap[1] + gap[2] * gap[2] + SOFTEN
                root = lax.rsqrt(square)
                factor = times[cell : cell + 1, :] * (root * root * root)
                for axis in range(3):
                    field_ref[axis * cells + cell, at, :] = factor * gap[axis]
            return carry

        lax.fori_loop(0, total * rows // 8, one, 0)

    ones = jnp.ones((8, atoms), jnp.float32)
    group = 32

    def pair_cell(cell):
        corner = (cell // 4) * 16 + ((cell // 2) % 2) * 4 + cell % 2
        for axis in range(3):
            row = around_ref[axis, pl.ds(corner + 21, 1), :]
            spread[axis] = jnp.transpose(jnp.broadcast_to(row, (atoms, atoms)))

        def one_group(n, carry):
            here = pl.ds(pl.multiple_of(n * group, group), group)
            mine = [spread[axis, here, :] for axis in range(3)]
            sums = [jnp.zeros((group, atoms), jnp.float32) for _ in range(3)]
            for dx in range(3):
                for dy in range(3):
                    for dz in range(3):
                        at = pl.ds(corner + dx * 16 + dy * 4 + dz, 1)
                        gap = [mine[axis] - around_ref[axis, at, :] for axis in range(3)]
                        power = around_ref[3, at, :] - (gap[0] * gap[0] + gap[1] * gap[1] + gap[2] * gap[2])
                        weight = jnp.exp2(power)
                        sums = [sums[axis] + weight * gap[axis] for axis in range(3)]
            for axis in range(3):
                spread[3 + axis, here, :] = sums[axis]
            return carry

        lax.fori_loop(0, atoms // group, one_group, 0)
        for axis in range(3):
            summed = lax.dot_general(
                ones, spread[3 + axis], (((1,), (1,)), ((), ())),
                precision=lax.Precision.HIGHEST, preferred_element_type=jnp.float32)
            pair_ref[axis, pl.ds(cell, 1), :] = summed[:1]

    def pair_cells(low_cell, high_cell):
        def one(cell, carry):
            pair_cell(cell)
            return carry

        lax.fori_loop(low_cell, high_cell, one, 0)

    run([(0, i, factor_of(0)) for i in middle])
    run([(0, i, factor_of(0)) for i in outer])
    post(1, 1)
    pass_on()
    count_atoms()

    for side in range(2):
        @pl.when(present[side])
        def _():
            finish((first_out, first_in), 0, side)
            row = (1, rows + 2)[side]
            columns = cut[1 - side]
            edge0[side, :, columns] = first_in[side]
            high0[row, :, columns], low0[row, :, columns] = split(first_in[side])

    ends = [0, rows - 1]
    beyond = [-1, rows]
    run([(0, i, factor_of(0)) for i in ends] + [(1, i, factor_of(1)) for i in middle])
    gather_around()
    gather_sites()
    make_field()

    for side in range(2):
        @pl.when(present[side])
        def _():
            finish((third_out, third_in), 1, side)
            finish((keep_out, keep_in), 2, side)
            row = (1, rows + 2)[side]
            columns = rest[1 - side]
            edge0[side, :, columns] = third_in[side]
            high0[row, :, columns], low0[row, :, columns] = split(third_in[side])
            edge_keep[side] = keep_in[side]

    def two_levels(t, carry):
        for k in range(2):
            slot = 1 - k
            level = 2 + 2 * t + k
            now = jnp.where(t == 0, factor_of(1 + k), factor_of(3 + k))
            before = jnp.where(t == 0, factor_of(k), factor_of(2 + k))
            after = jnp.where(t == 0, factor_of(2 + k), factor_of(4 + k))
            take_far(level - 2, 1 - slot)
            run([(slot, i, now) for i in outer] + [(1 - slot, i, before) for i in beyond])

            @pl.when(level < ITERS - 1)
            def _():
                post(level, 1 - slot)

            run([(slot, i, now) for i in ends] + [(1 - slot, i, after) for i in middle])
            pair_cells(2 * (level - 2), 2 * (level - 2) + 2)
        return carry

    lax.fori_loop(0, ITERS // 2 - 1, two_levels, 0)

    def store(i):
        return pltpu.make_async_copy(z0.at[i], out_ref.at[i], store_sem.at[i])

    def complete(i):
        for e in range(3):
            block = z0[i, e] * (1.5**ITERS)
            if e == W:
                block = block + half
                diag_ref[pl.ds(i, 1), :] = jnp.sum(jnp.where(eye, block, 0.0), axis=0, keepdims=True)
            z0[i, e] = block
        store(i).start()

    last = factor_of(ITERS - 1)
    run([(1, i, last) for i in outer])

    def inner(i, carry):
        complete(i)
        return carry

    lax.fori_loop(1, rows - 1, inner, 0)
    charge_out[...] = jnp.zeros((1, atoms), jnp.float32)
    take_far(ITERS - 2, 0)
    run([(0, i, factor_of(ITERS - 2)) for i in beyond])
    run([(1, i, last) for i in ends])
    complete(0)
    complete(rows - 1)

    def charge_copy(k, slot):
        peer = lax.rem(me + k, total)
        return pltpu.make_async_remote_copy(
            charge_out, charge_in.at[me if slot is None else peer], charge_send.at[k],
            charge_recv.at[me if slot is None else peer], device_id=place(peer), device_id_type=MESH)

    means = lax.dot_general(
        ones, diag_ref[...], (((1,), (1,)), ((), ())),
        precision=lax.Precision.HIGHEST, preferred_element_type=jnp.float32)[:1] * (1.0 / bs)
    charge_out[:, 0:rows] = sites_ref[3:4, :] - means

    def tell(k, carry):
        charge_copy(k, None).start()
        return carry

    lax.fori_loop(1, total, tell, 0)
    charge_square[pl.ds(me, 1), :] = charge_out[...]

    def hear(k, carry):
        charge_copy(k, None).wait_send()
        charge_copy(k, k).wait_recv()
        peer = lax.rem(me + k, total)
        charge_square[pl.ds(peer, 1), :] = charge_in[peer]
        return carry

    lax.fori_loop(1, total, hear, 0)
    for n in range(0, total, bs):
        turned = jnp.transpose(charge_square[n : n + bs, :])[:rows]
        for j in range(min(bs, total - n)):
            at = (n + j) * rows
            charge_rows[at : at + rows, :] = jnp.broadcast_to(turned[:, j : j + 1], (rows, atoms))

    def add_up(n, sums):
        sums = list(sums)
        for part in range(4):
            at = pl.ds(pl.multiple_of(n * 32 + part * 8, 8), 8)
            charge = charge_rows[at, :]
            sums = [total_so_far + charge * field_ref[k, at, :] for k, total_so_far in enumerate(sums)]
        return tuple(sums)

    sums = lax.fori_loop(0, total * rows // 32, add_up, (jnp.zeros((8, atoms), jnp.float32),) * (3 * cells))
    own_strength = strength * (1.0 / SCALE)
    for axis in range(3):
        for cell in range(cells):
            force = jnp.sum(sums[axis * cells + cell], axis=0, keepdims=True)
            here = slice(cell, cell + 1)
            force_ref[axis, here, :] = (
                pair_ref[axis, here, :] * own_strength[here] + EMBED * charges_ref[here, :] * force)

    def drain(i, carry):
        store(i).wait()
        return carry

    lax.fori_loop(0, rows, drain, 0)


def step(pattern, eps, counts, density, sites, positions, types, charges, lists, sizes):
    rows, band, bs = density.shape[:3]
    cells, atoms = charges.shape
    total = sizes[0] * sizes[1] * sizes[2]
    vmem, smem, anywhere = (pl.BlockSpec(memory_space=space) for space in (pltpu.VMEM, pltpu.SMEM, pl.ANY))

    def f32(*shape):
        return pltpu.VMEM(shape, jnp.float32)

    two, one = f32(2, bs, 2 * bs), f32(2, bs, bs)
    level_box = f32(ITERS - 1, 2, bs, 2 * bs)
    parts = pltpu.VMEM((rows + 4, bs, band * bs), jnp.bfloat16)
    edges, keeps = f32(2, bs, band * bs), f32(2, 8, bs)

    def copies(*shape):
        return pltpu.SemaphoreType.DMA(shape)

    return pl.pallas_call(
        functools.partial(step_kernel, sizes),
        out_shape=(
            jax.ShapeDtypeStruct(density.shape, jnp.float32),
            jax.ShapeDtypeStruct((3, cells, atoms), jnp.float32),
        ),
        in_specs=[smem, smem, smem, anywhere, vmem, vmem, vmem, vmem, vmem],
        out_specs=(anywhere, vmem),
        scratch_shapes=[
            f32(*density.shape), f32(*density.shape), parts, parts, parts, parts, edges, edges, keeps,
            pltpu.SMEM((rows, band), jnp.float32),
            keeps, keeps, two, two, one, one, level_box, level_box,
            f32(9, 2, 5, cells, atoms), f32(total // 2, 2, 8, atoms), f32(3, total * rows, atoms),
            f32(4, 64, atoms), f32(6, atoms, atoms), f32(3, cells, atoms), f32(total, cells, atoms),
            f32(3 * cells, total * rows, atoms),
            f32(rows, bs), f32(1, atoms), f32(total, 1, atoms), f32(-(-total // bs) * bs, atoms), f32(total * rows, atoms),
            copies(ITERS + 2, 2), copies(ITERS + 2, 2), copies(5), copies(rows), copies(9), copies(9),
            copies(total // 2), copies(total // 2), copies(total), copies(total),
        ],
        compiler_params=pltpu.CompilerParams(
            collective_id=0, has_side_effects=True, vmem_limit_bytes=60 * 1024 * 1024
        ),
        cost_estimate=pl.CostEstimate(
            flops=2 * 3 * 8 * 2 * ITERS * rows * bs**3, bytes_accessed=8 * density.size,
            transcendentals=27 * cells * atoms * atoms
        ),
    )(pattern, eps, counts, density, sites, positions, types, charges, lists)


def per_device(
    density, pattern, qm_sites, positions, atom_types, charges, eps_table, embed_atoms, embed_counts
):
    sizes = tuple(lax.axis_size(axis) for axis in ("qrow", "qcol", "grp"))
    atoms = charges.shape[-1]
    purified, force = step(
        pattern, eps_table, embed_counts[0], density, qm_sites, positions.reshape(3, -1, atoms),
        atom_types.reshape(-1, atoms), charges.reshape(-1, atoms), embed_atoms[0], sizes
    )
    return purified, force.reshape(positions.shape)


def solution(mesh):
    in_specs = (
        P(("qrow", "qcol", "grp"), None, None, None),
        P(("qrow", "qcol", "grp"), None),
        P(None, ("qrow", "qcol", "grp")),
        P(None, "qrow", "qcol", "grp", None),
        P("qrow", "qcol", "grp", None),
        P("qrow", "qcol", "grp", None),
        P(),
        P(("qrow", "qcol", "grp"), None, None),
        P(("qrow", "qcol", "grp"), None),
    )
    out_specs = (P(("qrow", "qcol", "grp"), None, None, None), P(None, "qrow", "qcol", "grp", None))
    return jax.shard_map(
        per_device, mesh=mesh, in_specs=in_specs, out_specs=out_specs, check_vma=False
    )
```

time: 101 us -> 88.6 us (0.88)
  starting transfers between devices: 18.4 us -> 0 us
  Pallas kernels: 63.9 us -> 81.8 us
  other arithmetic: 6.48 us -> 0 us
  waiting for transfers between devices: 5.29 us -> 0 us
    pallas_call x3 -> x1, Pallas kernels: 63.9 us -> 81.8 us  [step(): pl.pallas_call(functools.partial(step_kernel, sizes), out_shape=(jax.Shap...]
    all_to_all x1 -> x0, starting transfers between devices: 9.32 us -> none  [per_device(): lax.all_to_all(jnp.broadcast_to(table.reshape(1, -1), (device_count, tabl...]
    ppermute x6 -> x0, starting transfers between devices: 9.05 us -> none  [the longest x3 4.53 us: padded(): lax.ppermute(tail, axis, [(i, (i + 1) % count) for i in range(count)])]
    ppermute x6 -> x0, waiting for transfers between devices: 5.29 us -> none  [the longest x3 3.7 us: padded(): lax.ppermute(tail, axis, [(i, (i + 1) % count) for i in range(count)])]
    concatenate x5 -> x0, other arithmetic: 3 us -> none  [the longest x3 2.27 us: padded(): jnp.concatenate([lax.ppermute(tail, axis, [(i, (i + 1) % count) for i in...]
    unnamed x8 -> x5, local copies, waits for them, and re-layouts: 4.32 us -> 5.87 us
  transfers between devices with their start and end apart: 7 -> 0, of which waited for: 4 -> 0; matrix products, arithmetic and copies ran while one was open for 2% -> 0% of each run, Pallas kernels for 13% -> 0%
where the time goes in v1:
time: 88.6 us; the launch traced here: 88.3 us
  Pallas kernels  81.8 us (92%)
  local copies, waits for them, and re-layouts  5.87 us (7%)
    pallas_call x1, Pallas kernels, step(): pl.pallas_call(functools.partial(step_kernel, sizes), out_shape=(jax.Shap...  81.8 us
    unnamed x5, local copies, waits for them, and re-layouts  5.87 us

profile of v1, /device:TPU:0, one launch (start us, length us, event | category | flops | bytes accessed | tf_op | source)
XLA Modules:
  0.0 88.3 jit_solution(8410828641812833110)
XLA Ops:
  0.6 1.4 %copy.11.pattern_ref = s32[16,3]{1,0:T(8,128)} copy(s32[16,3]{0,1:T(4,128)} %param.10) | data formatting | bytes 384 | tf_op args[1]
  2.0 81.8 %shard_map.104 = (f32[16,3,128,128]{3,2,1,0:T(8,128)}, f32[3,8,128]{2,1,0:T(8,128)}) custom-call(s32[16,3]{1,0:T(8,128)} %copy.11.pattern_ref, f32[8]{0:T(128)} %eps_ref.1, s32[32]{0:T(128)} %bitcast.11, f32[16,3,128,128]{3,2,1,0:T(8,128)} %density_ref.1, f32[4,16]{1,0:T(4,128)} %sites_ref.1, f32[3,8,128]{2,1,0:T(8,128)} %bitcast.8, s32[8,128]{1,0:T(8,128)} %bitcast.9, ...), custom_call_target="tpu_custom_call" | custom-call | flops 19327352832 | bytes 6291456 | tf_op jit(solution)/shard_map/pallas_call | solution.py:536
  83.8 0.0 copy-start
  83.8 3.9 %copy.14 = f32[16,3,128,128]{3,2,1,0:T(8,128)} copy(f32[16,3,128,128]{3,2,1,0:T(8,128)} %get-tuple-element.8) | data formatting | bytes 6291456
  87.7 0.0 copy-done
  87.7 0.6 copy.15
Async XLA Ops:
  83.8 3.9 %copy-start = (f32[3,8,128]{2,1,0:T(8,128)S(1)}, f32[3,8,128]{2,1,0:T(8,128)}, u32[]{:S(2)}) copy-start(f32[3,8,128]{2,1,0:T(8,128)} %get-tuple-element.5) | copy-start | bytes 36868

commit v2 on v1

--- a/solution.py
+++ b/solution.py
@@ -16,6 +16,7 @@
 EMBED = 20.0
 SOFTEN = 1.0
 MESH = pl.DeviceIdType.MESH
+EARLY_CELLS = 4
 SCALE = math.sqrt(1.0 / (SIGMA_SQ * math.log(2.0)))
 
 
@@ -25,13 +26,13 @@
 
 
 def step_kernel(
-    sizes, pattern_ref, eps_ref, counts_ref, density_ref, sites_ref, positions_ref, types_ref, charges_ref, lists_ref,
-    out_ref, force_ref,
-    z0, z1, high0, high1, low0, low1, edge0, edge1, edge_keep, keep_ref,
+    sizes, pattern_ref, eps_ref, counts_ref, density_ref, sites_ref, positions_in, types_in, charges_in, lists_in,
+    z0, force_ref,
+    positions_ref, types_ref, charges_ref, lists_ref, z1, high0, high1, low0, low1, edge0, edge1, edge_keep, keep_ref,
     keep_out, keep_in, first_out, first_in, third_out, third_in, outbox, inbox,
-    blocks_ref, sites_in, site_rows, around_ref, spread, pair_ref, times_ref, field_ref,
+    blocks_ref, site_pair, sites_in, site_rows, around_ref, spread, pair_ref, times_ref, field_ref,
     diag_ref, charge_out, charge_in, charge_square, charge_rows,
-    send_sem, recv_sem, load_sem, store_sem, block_send, block_recv, site_send, site_recv, charge_send, charge_recv
+    send_sem, recv_sem, load_sem, block_send, block_recv, site_send, site_recv, charge_send, charge_recv
 ):
     rows, bs = density_ref.shape[0], density_ref.shape[2]
     n_row, n_col, n_grp = sizes
@@ -69,38 +70,49 @@
 
     barrier = pltpu.get_barrier_semaphore()
 
-    def greet(k, carry):
-        pl.semaphore_signal(barrier, inc=1, device_id=place(lax.rem(me + k, total)), device_id_type=MESH)
-        return carry
-
-    lax.fori_loop(1, total, greet, 0)
+    def wrapped(value, count):
+        return jnp.where(value >= count, value - count, value)
+
+    def each_peer(act):
+        def one(step_row, carry):
+            for step_col in range(n_col):
+                for step_grp in range(n_grp):
+                    where = (wrapped(at_row + step_row, n_row), wrapped(at_col + step_col, n_col), wrapped(at_grp + step_grp, n_grp))
+                    number = (step_row * n_col + step_col) * n_grp + step_grp
+                    peer = (where[0] * n_col + where[1]) * n_grp + where[2]
+                    if step_col == 0 and step_grp == 0:
+                        @pl.when(step_row > 0)
+                        def _():
+                            act(number, peer, where)
+                    else:
+                        act(number, peer, where)
+            return carry
+
+        lax.fori_loop(0, n_row, one, 0)
+
+    def greet(number, peer, where):
+        pl.semaphore_signal(barrier, inc=1, device_id=where, device_id_type=MESH)
+
+    each_peer(greet)
 
     near_rows, far_rows = (0, rows - 1), (1, rows - 2)
     loads = [pltpu.make_async_copy(density_ref.at[i], z0.at[i], load_sem.at[k]) for k, i in enumerate(near_rows + far_rows)]
     loads.append(pltpu.make_async_copy(density_ref.at[pl.ds(2, rows - 4)], z0.at[pl.ds(2, rows - 4)], load_sem.at[4]))
+    small = ((positions_in, positions_ref), (types_in, types_ref), (charges_in, charges_ref), (lists_in, lists_ref))
+    small = [pltpu.make_async_copy(*pair, load_sem.at[5 + k]) for k, pair in enumerate(small)]
+    loads = loads[:4] + small + loads[4:]
     for load in loads:
         load.start()
 
-    def keep_row(i, carry):
-        for e in range(3):
-            column = me * rows + i + e - W
-            inside = (column >= 0) & (column < total * rows) & (pattern_ref[i, e] > 0)
-            keep_ref[i, e] = jnp.where(inside, 1.0, 0.0).astype(jnp.float32)
-        return carry
-
-    lax.fori_loop(0, rows, keep_row, 0)
-
-    cells, atoms = charges_ref.shape
-    kinds = types_ref[...]
-    eps = jnp.zeros((cells, atoms), jnp.float32)
-    for kind in range(eps_ref.shape[0]):
-        eps = jnp.where(kinds == kind, eps_ref[kind], eps)
-    strength = jnp.sqrt(eps)
-    for axis in range(3):
-        blocks_ref[4, at_grp, axis] = positions_ref[axis]
-    blocks_ref[4, at_grp, 3] = jnp.log2(strength)
-    blocks_ref[4, at_grp, 4] = jnp.zeros((8, atoms), jnp.float32)
-    blocks_ref[4, at_grp, 4, 0:4, 0:rows] = sites_ref[...]
+    unit = lax.broadcasted_iota(jnp.int32, (rows, rows), 0) == lax.broadcasted_iota(jnp.int32, (rows, rows), 1)
+    for e in range(3):
+        column = me * rows + lax.broadcasted_iota(jnp.int32, (1, rows), 1) + e - W
+        kept = jnp.where((column >= 0) & (column < total * rows) & (pattern_ref[e : e + 1, :] > 0), 1.0, 0.0)
+        kept = jnp.sum(jnp.where(unit, jnp.broadcast_to(kept, (rows, rows)), 0.0), axis=1, keepdims=True)
+        keep_ref[e] = jnp.broadcast_to(kept, (rows, bs))
+
+    def keep_of(i, e):
+        return keep_ref[e, pl.ds(i, 1), :]
 
     eye = lax.broadcasted_iota(jnp.int32, (bs, bs), 0) == lax.broadcasted_iota(jnp.int32, (bs, bs), 1)
     half = jnp.where(eye, 0.5, 0.0)
@@ -109,7 +121,7 @@
         high[slot][row + 2], low[slot][row + 2] = split(value)
 
     def masked(i):
-        blocks = [z0[i, e] if e == W else z0[i, e] * keep_ref[i, e] for e in range(3)]
+        blocks = [z0[i, e] if e == W else z0[i, e] * keep_of(i, e) for e in range(3)]
         blocks[W] = blocks[W] - half
         for e in range(3):
             z0[i, e] = blocks[e]
@@ -126,21 +138,39 @@
         third_out[side] = near[side][:, rest[side]]
         outbox[0, side] = far[side][:, cut[side]]
         for e in range(3):
-            keep_out[side, e : e + 1, :] = jnp.full((1, bs), keep_ref[(rows - 1) * side, e], jnp.float32)
+            keep_out[side, e : e + 1, :] = keep_of((rows - 1) * side, e)
 
     pl.semaphore_wait(barrier, total - 1)
     send((first_out, first_in), 0)
-    send(level_boxes(0), 3)
-    send((third_out, third_in), 1)
-    send((keep_out, keep_in), 2)
-
-    across = pltpu.make_async_remote_copy(
-        blocks_ref.at[4, at_grp], blocks_ref.at[4, at_grp], block_send.at[4], block_recv.at[4],
+
+    cells, atoms = charges_ref.shape
+    for load in small:
+        load.wait()
+    kinds = types_ref[...]
+    eps = jnp.zeros((cells, atoms), jnp.float32)
+    for kind in range(eps_ref.shape[0]):
+        eps = jnp.where(kinds == kind, eps_ref[kind], eps)
+    strength = jnp.sqrt(eps)
+    powers = jnp.log2(strength)
+    for x in range(2):
+        for y in range(2):
+            pick = slice(4 * x + 2 * y, 4 * x + 2 * y + 2)
+            tile = [positions_ref[axis, pick, :] for axis in range(3)] + [powers[pick]]
+            blocks_ref[4, x, y, at_grp] = jnp.concatenate(tile, axis=0)
+    site_pair[0] = jnp.zeros((8, atoms), jnp.float32)
+    site_pair[0, :, 0:rows] = jnp.concatenate(
+        [jnp.where(at_grp == g, sites_ref[...], 0.0) for g in range(n_grp)], axis=0)
+
+    def across(g):
+        return pltpu.make_async_remote_copy(
+            blocks_ref.at[4, :, :, g], blocks_ref.at[4, :, :, g], block_send.at[4], block_recv.at[4],
+            device_id=(at_row, at_col, 1 - at_grp), device_id_type=MESH)
+
+    across_sites = pltpu.make_async_remote_copy(
+        site_pair.at[0], site_pair.at[1], block_send.at[9], block_recv.at[9],
         device_id=(at_row, at_col, 1 - at_grp), device_id_type=MESH)
-    across_in = pltpu.make_async_remote_copy(
-        blocks_ref.at[4, 1 - at_grp], blocks_ref.at[4, 1 - at_grp], block_send.at[4], block_recv.at[4],
-        device_id=(at_row, at_col, 1 - at_grp), device_id_type=MESH)
-    across.start()
+    across(at_grp).start()
+    across_sites.start()
 
     for side, row in ((0, 0), (1, rows - 1)):
         put(0, row, near[side])
@@ -155,7 +185,7 @@
                 high[slot][row] = blank
                 low[slot][row] = blank
 
-    loads[4].wait()
+    loads[-1].wait()
 
     def fill(i, carry):
         put(0, i, masked(i))
@@ -185,7 +215,7 @@
 
     def masks(i):
         if own(i):
-            return [keep_ref[i, e] for e in range(3)]
+            return [keep_of(i, e) for e in range(3)]
         return [edge_keep[0 if i < 0 else 1, e : e + 1, :] for e in range(3)]
 
     def squared(slot, i, factor, keep):
@@ -238,8 +268,9 @@
     def around_copy(k):
         step_row, step_col = k // 3 - 1, k % 3 - 1
         target = (lax.rem(at_row + step_row + n_row, n_row), lax.rem(at_col + step_col + n_col, n_col), at_grp)
+        xs, ys = ((pl.ds(0, 1), pl.ds(0, 2), pl.ds(1, 1))[step + 1] for step in (step_row, step_col))
         return pltpu.make_async_remote_copy(
-            blocks_ref.at[4], blocks_ref.at[8 - k], block_send.at[k], block_recv.at[8 - k],
+            blocks_ref.at[4, xs, ys], blocks_ref.at[8 - k, xs, ys], block_send.at[k], block_recv.at[8 - k],
             device_id=target, device_id_type=MESH)
 
     def site_copy(k, slot):
@@ -252,12 +283,12 @@
     others = [k for k in range(9) if k != 4]
 
     def pass_on():
-        across.wait_send()
-        across_in.wait_recv()
+        across(at_grp).wait_send()
+        across(1 - at_grp).wait_recv()
+        across_sites.wait()
         for k in others:
             around_copy(k).start()
-        for g in range(n_grp):
-            sites_in[home, g] = blocks_ref[4, g, 4]
+        sites_in[home] = site_pair[0] + site_pair[1]
 
         def one(k, carry):
             site_copy(k, None).start()
@@ -274,12 +305,12 @@
                 for z in range(-1, 3):
                     k = (x // 2 + 1) * 3 + y // 2 + 1
                     g = at_grp if 0 <= z < 2 else 1 - at_grp
-                    cell = (x % 2) * 4 + (y % 2) * 2 + z % 2
                     at = (x + 1) * 16 + (y + 1) * 4 + z + 1
+                    tile = blocks_ref.at[k, x % 2, y % 2, g]
                     for axis, shift in enumerate((x, y, z)):
-                        row = blocks_ref[k, g, axis, cell : cell + 1, :]
-                        around_ref[axis, at : at + 1, :] = (row + float(shift)) * SCALE
-                    around_ref[3, at : at + 1, :] = blocks_ref[k, g, 3, cell : cell + 1, :]
+                        from_row = 2 * axis + z % 2
+                        around_ref[axis, at : at + 1, :] = (tile[from_row : from_row + 1, :] + float(shift)) * SCALE
+                    around_ref[3, at : at + 1, :] = tile[6 + z % 2 : 7 + z % 2, :]
 
     def gather_sites():
         def one(k, carry):
@@ -288,15 +319,15 @@
             return carry
 
         lax.fori_loop(1, n_row * n_col, one, 0)
-        per = bs // 8
+        per = bs // 4
 
         def some(n, carry):
-            tiles = sites_in[pl.ds(n * (per // n_grp), per // n_grp)].reshape(bs, atoms)
+            tiles = sites_in[pl.ds(n * (per // 2), per // 2)].reshape(bs, atoms)
             turned = jnp.transpose(tiles)[:rows]
             for j in range(per):
                 at = pl.ds(pl.multiple_of((n * per + j) * rows, rows), rows)
                 for axis in range(3):
-                    site_rows[axis, at, :] = jnp.broadcast_to(turned[:, j * 8 + axis : j * 8 + axis + 1], (rows, atoms))
+                    site_rows[axis, at, :] = jnp.broadcast_to(turned[:, j * 4 + axis : j * 4 + axis + 1], (rows, atoms))
             return carry
 
         lax.fori_loop(0, total // per, some, 0)
@@ -381,6 +412,9 @@
         lax.fori_loop(low_cell, high_cell, one, 0)
 
     run([(0, i, factor_of(0)) for i in middle])
+    send(level_boxes(0), 3)
+    send((third_out, third_in), 1)
+    send((keep_out, keep_in), 2)
     run([(0, i, factor_of(0)) for i in outer])
     post(1, 1)
     pass_on()
@@ -428,13 +462,10 @@
                 post(level, 1 - slot)
 
             run([(slot, i, now) for i in ends] + [(1 - slot, i, after) for i in middle])
-            pair_cells(2 * (level - 2), 2 * (level - 2) + 2)
+            pair_cells(level - 2, level - 1)
         return carry
 
     lax.fori_loop(0, ITERS // 2 - 1, two_levels, 0)
-
-    def store(i):
-        return pltpu.make_async_copy(z0.at[i], out_ref.at[i], store_sem.at[i])
 
     def complete(i):
         for e in range(3):
@@ -443,7 +474,6 @@
                 block = block + half
                 diag_ref[pl.ds(i, 1), :] = jnp.sum(jnp.where(eye, block, 0.0), axis=0, keepdims=True)
             z0[i, e] = block
-        store(i).start()
 
     last = factor_of(ITERS - 1)
     run([(1, i, last) for i in outer])
@@ -460,32 +490,26 @@
     complete(0)
     complete(rows - 1)
 
-    def charge_copy(k, slot):
-        peer = lax.rem(me + k, total)
+    def charge_copy(number, slot, where):
         return pltpu.make_async_remote_copy(
-            charge_out, charge_in.at[me if slot is None else peer], charge_send.at[k],
-            charge_recv.at[me if slot is None else peer], device_id=place(peer), device_id_type=MESH)
+            charge_out, charge_in.at[slot], charge_send.at[number], charge_recv.at[slot],
+            device_id=where, device_id_type=MESH)
 
     means = lax.dot_general(
         ones, diag_ref[...], (((1,), (1,)), ((), ())),
         precision=lax.Precision.HIGHEST, preferred_element_type=jnp.float32)[:1] * (1.0 / bs)
     charge_out[:, 0:rows] = sites_ref[3:4, :] - means
 
-    def tell(k, carry):
-        charge_copy(k, None).start()
-        return carry
-
-    lax.fori_loop(1, total, tell, 0)
+    each_peer(lambda number, peer, where: charge_copy(number, me, where).start())
     charge_square[pl.ds(me, 1), :] = charge_out[...]
-
-    def hear(k, carry):
-        charge_copy(k, None).wait_send()
-        charge_copy(k, k).wait_recv()
-        peer = lax.rem(me + k, total)
+    pair_cells(EARLY_CELLS, cells)
+
+    def hear(number, peer, where):
+        charge_copy(number, me, where).wait_send()
+        charge_copy(number, peer, where).wait_recv()
         charge_square[pl.ds(peer, 1), :] = charge_in[peer]
-        return carry
-
-    lax.fori_loop(1, total, hear, 0)
+
+    each_peer(hear)
     for n in range(0, total, bs):
         turned = jnp.transpose(charge_square[n : n + bs, :])[:rows]
         for j in range(min(bs, total - n)):
@@ -509,18 +533,12 @@
             force_ref[axis, here, :] = (
                 pair_ref[axis, here, :] * own_strength[here] + EMBED * charges_ref[here, :] * force)
 
-    def drain(i, carry):
-        store(i).wait()
-        return carry
-
-    lax.fori_loop(0, rows, drain, 0)
-
 
 def step(pattern, eps, counts, density, sites, positions, types, charges, lists, sizes):
     rows, band, bs = density.shape[:3]
     cells, atoms = charges.shape
     total = sizes[0] * sizes[1] * sizes[2]
-    vmem, smem, anywhere = (pl.BlockSpec(memory_space=space) for space in (pltpu.VMEM, pltpu.SMEM, pl.ANY))
+    vmem, smem, hbm = (pl.BlockSpec(memory_space=space) for space in (pltpu.VMEM, pltpu.SMEM, pltpu.HBM))
 
     def f32(*shape):
         return pltpu.VMEM(shape, jnp.float32)
@@ -539,27 +557,28 @@
             jax.ShapeDtypeStruct(density.shape, jnp.float32),
             jax.ShapeDtypeStruct((3, cells, atoms), jnp.float32),
         ),
-        in_specs=[smem, smem, smem, anywhere, vmem, vmem, vmem, vmem, vmem],
-        out_specs=(anywhere, vmem),
+        in_specs=[vmem, smem, smem, hbm, vmem, hbm, hbm, hbm, hbm],
+        out_specs=(vmem, vmem),
         scratch_shapes=[
-            f32(*density.shape), f32(*density.shape), parts, parts, parts, parts, edges, edges, keeps,
-            pltpu.SMEM((rows, band), jnp.float32),
+            f32(*positions.shape), pltpu.VMEM(types.shape, jnp.int32), f32(*charges.shape), pltpu.VMEM(lists.shape, jnp.int32),
+            f32(*density.shape), parts, parts, parts, parts, edges, edges, keeps,
+            f32(band, rows, bs),
             keeps, keeps, two, two, one, one, level_box, level_box,
-            f32(9, 2, 5, cells, atoms), f32(total // 2, 2, 8, atoms), f32(3, total * rows, atoms),
+            f32(9, 2, 2, 2, 8, atoms), f32(2, 8, atoms), f32(total // 2, 8, atoms), f32(3, total * rows, atoms),
             f32(4, 64, atoms), f32(6, atoms, atoms), f32(3, cells, atoms), f32(total, cells, atoms),
             f32(3 * cells, total * rows, atoms),
             f32(rows, bs), f32(1, atoms), f32(total, 1, atoms), f32(-(-total // bs) * bs, atoms), f32(total * rows, atoms),
-            copies(ITERS + 2, 2), copies(ITERS + 2, 2), copies(5), copies(rows), copies(9), copies(9),
+            copies(ITERS + 2, 2), copies(ITERS + 2, 2), copies(9), copies(10), copies(10),
             copies(total // 2), copies(total // 2), copies(total), copies(total),
         ],
         compiler_params=pltpu.CompilerParams(
-            collective_id=0, has_side_effects=True, vmem_limit_bytes=60 * 1024 * 1024
+            collective_id=0, has_side_effects=True, vmem_limit_bytes=26 * 1024 * 1024 + total * rows * atoms * 4 * (3 * cells + 4)
         ),
         cost_estimate=pl.CostEstimate(
             flops=2 * 3 * 8 * 2 * ITERS * rows * bs**3, bytes_accessed=8 * density.size,
             transcendentals=27 * cells * atoms * atoms
         ),
-    )(pattern, eps, counts, density, sites, positions, types, charges, lists)
+    )(*(pltpu.with_memory_space_constraint(x, pltpu.HBM) for x in (pattern, eps, counts, density, sites, positions, types, charges, lists)))
 
 
 def per_device(
@@ -568,7 +587,7 @@
     sizes = tuple(lax.axis_size(axis) for axis in ("qrow", "qcol", "grp"))
     atoms = charges.shape[-1]
     purified, force = step(
-        pattern, eps_table, embed_counts[0], density, qm_sites, positions.reshape(3, -1, atoms),
+        pattern.T, eps_table, embed_counts[0], density, qm_sites, positions.reshape(3, -1, atoms),
         atom_types.reshape(-1, atoms), charges.reshape(-1, atoms), embed_atoms[0], sizes
     )
     return purified, force.reshape(positions.shape)

time: 88.6 us -> 68.3 us (0.77)
  Pallas kernels: 81.8 us -> 65.2 us
  local copies, waits for them, and re-layouts: 5.87 us -> 2.27 us
    pallas_call x1, Pallas kernels: 81.8 us -> 65.2 us  [step(): pl.pallas_call(functools.partial(step_kernel, sizes), out_shape=(jax.Shap...]
    unnamed x5 -> x2, local copies, waits for them, and re-layouts: 5.87 us -> 2.27 us
where the time goes in v2:
time: 68.3 us; the launch traced here: 68.1 us
  Pallas kernels  65.2 us (95%)
  local copies, waits for them, and re-layouts  2.27 us (3%)
    pallas_call x1, Pallas kernels, step(): pl.pallas_call(functools.partial(step_kernel, sizes), out_shape=(jax.Shap...  65.2 us
    unnamed x2, local copies, waits for them, and re-layouts  2.27 us

profile of v2, /device:TPU:0, one launch (start us, length us, event | category | flops | bytes accessed | tf_op | source)
XLA Modules:
  0.0 68.1 jit_solution(1680719317122736076)
XLA Ops:
  0.6 65.2 %shard_map.104 = (f32[16,3,128,128]{3,2,1,0:T(8,128)S(1)}, f32[3,8,128]{2,1,0:T(8,128)S(1)}) custom-call(s32[3,16]{1,0:T(4,128)} %bitcast.12, f32[8]{0:T(128)} %eps_ref.1, s32[32]{0:T(128)} %bitcast.13, f32[16,3,128,128]{3,2,1,0:T(8,128)} %density_ref.1, f32[4,16]{1,0:T(4,128)} %sites_ref.1, f32[3,8,128]{2,1,0:T(8,128)} %bitcast.9, s32[8,128]{1,0:T(8,128)} %bitcast.10, ...), custom_call_target="tpu_custom_call" | custom-call | flops 19327352832 | bytes 6291456 | tf_op jit(solution)/shard_map/pallas_call | solution.py:554
  65.8 1.7 %copy.13 = f32[16,3,128,128]{3,2,1,0:T(8,128)} copy(f32[16,3,128,128]{3,2,1,0:T(8,128)S(1)} %get-tuple-element.8) | data formatting | bytes 6291456
  67.5 0.6 copy.14

commit v3 on v2

--- a/solution.py
+++ b/solution.py
@@ -416,7 +416,6 @@
     send((third_out, third_in), 1)
     send((keep_out, keep_in), 2)
     run([(0, i, factor_of(0)) for i in outer])
-    post(1, 1)
     pass_on()
     count_atoms()
 
@@ -429,6 +428,7 @@
             edge0[side, :, columns] = first_in[side]
             high0[row, :, columns], low0[row, :, columns] = split(first_in[side])
 
+    post(1, 1)
     ends = [0, rows - 1]
     beyond = [-1, rows]
     run([(0, i, factor_of(0)) for i in ends] + [(1, i, factor_of(1)) for i in middle])
@@ -454,15 +454,16 @@
             now = jnp.where(t == 0, factor_of(1 + k), factor_of(3 + k))
             before = jnp.where(t == 0, factor_of(k), factor_of(2 + k))
             after = jnp.where(t == 0, factor_of(2 + k), factor_of(4 + k))
-            take_far(level - 2, 1 - slot)
-            run([(slot, i, now) for i in outer] + [(1 - slot, i, before) for i in beyond])
+            run([(slot, i, now) for i in outer])
 
             @pl.when(level < ITERS - 1)
             def _():
                 post(level, 1 - slot)
 
-            run([(slot, i, now) for i in ends] + [(1 - slot, i, after) for i in middle])
             pair_cells(level - 2, level - 1)
+            take_far(level - 2, 1 - slot)
+            run([(1 - slot, i, before) for i in beyond] + [(1 - slot, i, after) for i in middle[::2]])
+            run([(slot, i, now) for i in ends] + [(1 - slot, i, after) for i in middle[1::2]])
         return carry
 
     lax.fori_loop(0, ITERS // 2 - 1, two_levels, 0)

time: 68.3 us -> 66.8 us (0.978); the launches traced: 68.1 us -> 65.6 us
  Pallas kernels: 65.2 us -> 62.7 us
    pallas_call x1, Pallas kernels: 65.2 us -> 62.7 us  [step(): pl.pallas_call(functools.partial(step_kernel, sizes), out_shape=(jax.Shap...]
where the time goes in v3:
time: 66.8 us; the launch traced here: 65.6 us
  Pallas kernels  62.7 us (94%)
  local copies, waits for them, and re-layouts  2.27 us (3%)
    pallas_call x1, Pallas kernels, step(): pl.pallas_call(functools.partial(step_kernel, sizes), out_shape=(jax.Shap...  62.7 us
    unnamed x2, local copies, waits for them, and re-layouts  2.27 us

profile of v3, /device:TPU:0, one launch (start us, length us, event | category | flops | bytes accessed | tf_op | source)
XLA Modules:
  0.0 65.6 jit_solution(7281482597592085513)
XLA Ops:
  0.6 62.7 %shard_map.104 = (f32[16,3,128,128]{3,2,1,0:T(8,128)S(1)}, f32[3,8,128]{2,1,0:T(8,128)S(1)}) custom-call(s32[3,16]{1,0:T(4,128)} %bitcast.12, f32[8]{0:T(128)} %eps_ref.1, s32[32]{0:T(128)} %bitcast.13, f32[16,3,128,128]{3,2,1,0:T(8,128)} %density_ref.1, f32[4,16]{1,0:T(4,128)} %sites_ref.1, f32[3,8,128]{2,1,0:T(8,128)} %bitcast.9, s32[8,128]{1,0:T(8,128)} %bitcast.10, ...), custom_call_target="tpu_custom_call" | custom-call | flops 19327352832 | bytes 6291456 | tf_op jit(solution)/shard_map/pallas_call | solution.py:555
  63.3 1.7 %copy.13 = f32[16,3,128,128]{3,2,1,0:T(8,128)} copy(f32[16,3,128,128]{3,2,1,0:T(8,128)S(1)} %get-tuple-element.8) | data formatting | bytes 6291456
  65.0 0.6 copy.14
